TPU v7x, 256 devices: a whole 4x4x8 slice. The times are simulated.
256 devices in a mesh: gx: 32 (over y, x, core), gy: 8 (over z).
Axes of the slice: x: 4, y: 4, z: 8, core: 2. Of those that a mesh axis runs over, the one named last changes fastest.
Arguments:
- blocks: float32 [32, 8, 8, 128, 128], P('gx', 'gy')
- face_maps: float32 [6, 128, 64], replicated, may hold values from -0.18 to 0.18
- couple: float32 [32, 8, 8, 128, 128], P('gx', 'gy'), may hold values from -0.5 to 0.5
- order_one: int32 [32, 8, 8, 128], P('gx', 'gy'), may hold values from 0 to 127, each once within a row
- count_one: int32 [32, 8, 8], P('gx', 'gy'), may hold values from 16 to 64, as said below
- merge_map: int32 [32, 8, 8], P('gx', 'gy'), may hold values from 0 to 7, as said below
- order_two: int32 [32, 8, 4, 128], P('gx', 'gy'), may hold values from 0 to 127, each once within a row
- count_two: int32 [32, 8, 4], P('gx', 'gy'), may hold values from 16 to 64, as said below
Outputs:
- skeleton_one: float32 [32, 8, 8, 64, 64], P('gx', 'gy')
- skeleton_two: float32 [32, 8, 4, 64, 64], P('gx', 'gy')
Inputs may be any that keep to these rules, and one draw needn't show every extreme that they name: Each row of order_one is a permutation of 0 to 127. Each row of order_two is a permutation of 0 to 127. `count_one`: counts are larger on average in the upper half of the first dimension. `count_two`: counts are larger on average in the upper half of the first dimension. For each pair of first-dimension positions 2p and 2p+1 and each y, merge_map at 2p is a permutation of the slots and merge_map at 2p+1 is its inverse.
All inputs are finite; a program needn't handle non-finite values.
Results may differ from a plain program's by a relative error of at most 0.0003.
Values sent between devices are 32-bit elements; how exact they have to be, the bound alone decides.
A program may use at most 64 MiB of HBM per device.

v0:
```python
import functools

import jax
import jax.numpy as jnp
from jax import lax
from jax.experimental import pallas as pl
from jax.experimental.pallas import tpu as pltpu
from jax.sharding import PartitionSpec as P

MESH = pl.DeviceIdType.MESH
BF = jnp.bfloat16
F32 = jnp.float32
NN = (((1,), (0,)), ((), ()))
NT = (((1,), (1,)), ((), ()))
K = 64
M = 128


def dot(left, right, dims):
    return lax.dot_general(left, right, dims, preferred_element_type=F32)


def split(x):
    high = x.astype(BF)
    low = (x - high.astype(F32)).astype(BF)
    return high, low


def lanes(*parts):
    return jnp.concatenate(parts, axis=1)


def rows(*parts):
    return jnp.concatenate(parts, axis=0)


def nn3(left, right):
    lh, ll = left
    rh, rl = right
    return dot(lanes(lh, ll, lh), rows(rh, rh, rl), NN)


def nt3(left, right):
    lh, ll = left
    rh, rl = right
    return dot(lanes(lh, ll, lh), lanes(rh, rh, rl), NT)


def iota(shape, dim):
    return lax.broadcasted_iota(jnp.int32, shape, dim)


def invert(pairs):
    count = len(pairs)
    left = iota((1, M), 1) < K
    scales = []
    tiles = [[] for _ in range(8)]
    for n in pairs:
        top = jnp.max(n, axis=0, keepdims=True)
        first = jnp.max(jnp.where(left, top, 0.0), axis=1, keepdims=True)
        second = jnp.max(jnp.where(left, 0.0, top), axis=1, keepdims=True)
        scale = 1.0 / jnp.where(left, first, second)
        scales.append(scale)
        n = n * scale
        for i in range(8):
            tiles[i].append(n[8 * i : 8 * i + 8])
    tiles = [jnp.stack(t) for t in tiles]
    lane = iota((count, 8, M), 2)
    half = jnp.where(lane >= K, K, 0)
    within = iota((count, 1, M), 2) % K
    sub = iota((count, 8, M), 1)

    def body(t, tiles):
        tiles = list(tiles)
        for q in range(8):
            step = t * 8 + q
            place = half + step
            cols = [jnp.take_along_axis(x, place, axis=2, mode="promise_in_bounds") for x in tiles]
            row = tiles[0][:, q : q + 1, :]
            inverse = 1.0 / cols[0][:, q : q + 1, :]
            row = jnp.where(within == step, 1.0 + inverse, row * inverse)
            cols[0] = jnp.where(sub == q, cols[0] - 1.0, cols[0])
            tiles = [x - c * row for x, c in zip(tiles, cols)]
        return tuple(tiles[1:] + tiles[:1])

    tiles = lax.fori_loop(0, 8, body, tuple(tiles))
    return [
        rows(*[tiles[i][p] for i in range(8)]) * scales[p] for p in range(count)
    ]


def skeletonize(read_block, turn_of, counts, write):
    boxes = len(counts)
    row_of = iota((K, M), 0)
    lane_of = iota((K, M), 1)
    left = lane_of < K
    diagonal = (lane_of % K) == row_of
    normals, sides = [], []
    for b in range(0, boxes, 2):
        halves = []
        for i in (0, 1):
            c = counts[b + i]
            ah, al = split(read_block(b + i))
            turn = turn_of(b + i)
            turned = split(dot(lanes(turn, turn), lanes(ah, al), NT))
            skel = tuple(jnp.where(row_of < c, x[:K], jnp.zeros_like(x[:K])) for x in turned)
            gram = nt3(skel, turned)
            sides.append(jnp.where(lane_of >= c, gram, 0.0))
            normal = jnp.where(lane_of < c, gram, 0.0)
            if i == 1:
                normal = pltpu.roll(normal, K, 1)
                c_here = counts[b + 1]
            halves.append(normal)
        padded = jnp.where(row_of >= jnp.where(left, counts[b], counts[b + 1]), 1.0, 0.0)
        normals.append(
            jnp.where(left, halves[0], halves[1]) + jnp.where(diagonal, padded, 0.0)
        )
    inverses = invert(normals)
    for b in range(0, boxes, 2):
        zero = jnp.zeros((K, M), BF)
        firsts, seconds = split(sides[b]), split(sides[b + 1])
        right = tuple(
            rows(lanes(f, zero), lanes(zero, s)) for f, s in zip(firsts, seconds)
        )
        interp = nn3(split(inverses[b // 2]), right)
        for i in (0, 1):
            c = counts[b + i]
            keep = jnp.where((lane_of == row_of) & (row_of < c), 1.0, 0.0)
            short = split(interp[:, M * i : M * i + M] + keep)
            turn = turn_of(b + i)
            weights = dot(lanes(*short), rows(turn, turn), NN)
            parts = split(weights)
            applied = split(nn3(parts, split(read_block(b + i))))
            twice = tuple(rows(x, x) for x in parts)
            pad = jnp.where(diagonal & (row_of >= c), 1.0, 0.0)
            write(b + i, nt3(applied, twice) + pad, weights)


def kernel(
    sizes,
    blocks_hbm, faces_hbm, couple_hbm, order_one, count_one, merge_map, order_two, count_two,
    out_one, out_two,
    a_ref, face_ref, c_ref, turn_ref, own_ref, near_ref, send_c, near_c, mixed_ref,
    q_ref, child_ref, send_child, level_ref, parent_ref,
    load_sems, send_sems, recv_sems,
):
    nx, ny = sizes
    gx, gy = lax.axis_index("gx"), lax.axis_index("gy")
    odd = gx % 2
    boxes = 8
    parents = 4

    loads = [pltpu.make_async_copy(blocks_hbm.at[0, 0, b], a_ref.at[b], load_sems.at[b]) for b in range(boxes)]
    load_face = pltpu.make_async_copy(faces_hbm, face_ref, load_sems.at[8])
    load_c = pltpu.make_async_copy(couple_hbm.at[0, 0], c_ref, load_sems.at[9])
    for load in loads:
        load.start()
    load_face.start()
    load_c.start()

    barrier = pltpu.get_barrier_semaphore()
    sides = (
        (gx > 0, {"gx": gx - 1, "gy": gy}, 1),
        (gx < nx - 1, {"gx": gx + 1, "gy": gy}, 0),
        (gy > 0, {"gx": gx, "gy": gy - 1}, 3),
        (gy < ny - 1, {"gx": gx, "gy": gy + 1}, 2),
    )
    partner = {"gx": gx + 1 - 2 * odd, "gy": gy}
    for there, where, _ in sides:
        @pl.when(there)
        def _(where=where):
            pl.semaphore_signal(barrier, inc=1, device_id=where, device_id_type=MESH)

    orders = rows(
        order_one[0, 0].astype(F32), order_two[0, 0].astype(F32), jnp.zeros((4, M), F32)
    ).T
    lane = iota((M, M), 1).astype(F32)
    for b in range(boxes + parents):
        turn_ref[b] = jnp.where(orders[:, b : b + 1] == lane, 1.0, 0.0).astype(BF)

    row_of = iota((K, M), 0)
    lane_of = iota((K, M), 1)
    left = lane_of < K
    counts = [count_one[0, 0, b] for b in range(boxes)]

    def copies(part):
        got = []
        for d, (there, where, face) in enumerate(sides):
            got.append((there, pltpu.make_async_remote_copy(
                src_ref=own_ref.at[part],
                dst_ref=near_ref.at[face, part],
                send_sem=send_sems.at[2 * d + part],
                recv_sem=recv_sems.at[2 * face + part],
                device_id=where,
                device_id_type=MESH,
            )))
        return got

    for part in range(2):
        for b in range(4 * part, 4 * part + 4, 2):
            halves = []
            for i in (0, 1):
                loads[b + i].wait()
                turn = turn_ref[b + i]
                ah, al = split(a_ref[b + i])
                picked = split(dot(lanes(turn[:K], turn[:K]), rows(ah, al), NN))
                other = turn if i == 0 else rows(turn[K:], turn[:K])
                halves.append(dot(lanes(*picked), lanes(other, other), NT))
            c = jnp.where(left, counts[b], counts[b + 1])
            s = jnp.where(left, halves[0], halves[1])
            s = jnp.where((row_of < c) & (lane_of % K < c), s, 0.0)
            own_ref[part, (b % 4) // 2 * K : (b % 4) // 2 * K + K, :] = s
        if part == 0:
            pl.semaphore_wait(
                barrier,
                (gx + nx - 1) // nx + (2 * nx - 2 - gx) // nx
                + (gy + ny - 1) // ny + (2 * ny - 2 - gy) // ny,
            )
        for there, copy in reversed(copies(part)):
            @pl.when(there)
            def _(copy=copy):
                copy.start()

    m = [merge_map[0, 0, b] for b in range(boxes)]
    found = []
    for k in range(boxes):
        at = jnp.int32(0)
        for b in range(1, boxes):
            at = jnp.where(m[b] == k, b, at)
        found.append(at)
    is_odd = odd == 1
    send_box = [jnp.where(is_odd, found[k], k + 4) for k in range(parents)]
    keep_box = [jnp.where(is_odd, found[k + 4], k) for k in range(parents)]

    load_c.wait()
    for k in range(parents):
        send_c[k] = c_ref[send_box[k]]
    couple_copy = pltpu.make_async_remote_copy(
        src_ref=send_c, dst_ref=near_c, send_sem=send_sems.at[8], recv_sem=recv_sems.at[8],
        device_id=partner, device_id_type=MESH,
    )
    couple_copy.start()

    for there, _, face in sides:
        @pl.when(jnp.logical_not(there))
        def _(face=face):
            near_ref[face ^ 1] = jnp.zeros((2, 2 * K, M), F32)

    load_face.wait()

    def project(f, source):
        face = split(face_ref[f])
        zero = jnp.zeros((M, K), BF)
        right = tuple(rows(lanes(x, zero), lanes(zero, x)) for x in face)
        return nt3(split(source), right)

    for f in (4, 5):
        q = project(f, own_ref[...].reshape(4 * K, M))
        for b in range(boxes):
            p, i = b // 2, b % 2
            n = b + 1 if f == 4 else b - 1
            if 0 <= n < boxes:
                q_ref[n // 2, f * K : f * K + K, M * (n % 2) : M * (n % 2) + M] = (
                    q[p * K : p * K + K, M * i : M * i + M]
                )
        edge = 0 if f == 4 else boxes - 1
        q_ref[edge // 2, f * K : f * K + K, M * (edge % 2) : M * (edge % 2) + M] = jnp.zeros((K, M), F32)

    for f in range(4):
        there = sides[f][0]
        for part in range(2):
            @pl.when(there)
            def _(f=f, part=part):
                pltpu.make_async_remote_copy(
                    src_ref=own_ref.at[part],
                    dst_ref=near_ref.at[f, part],
                    send_sem=send_sems.at[2 * f + part],
                    recv_sem=recv_sems.at[2 * f + part],
                    device_id=sides[f][1],
                    device_id_type=MESH,
                ).wait_recv()
        q = project(f, near_ref[f].reshape(4 * K, M))
        for p in range(4):
            q_ref[p, f * K : f * K + K, :] = q[p * K : p * K + K]

    all_faces = split(lanes(*[face_ref[f] for f in range(6)]))
    for p in range(4):
        d = nn3(all_faces, split(q_ref[p]))
        for i in (0, 1):
            a_ref[2 * p + i] = a_ref[2 * p + i] - d[:, M * i : M * i + M]

    def write_one(b, z, w):
        level_ref[b, :K] = z
        level_ref[b, K:] = w
        out_one[0, 0, b] = z[:, :K]

    skeletonize(lambda b: a_ref[b], lambda b: turn_ref[b], counts, write_one)

    for k in range(parents):
        send_child[k] = level_ref[send_box[k]]
    child_copy = pltpu.make_async_remote_copy(
        src_ref=send_child, dst_ref=child_ref.at[odd], send_sem=send_sems.at[9],
        recv_sem=recv_sems.at[9], device_id=partner, device_id_type=MESH,
    )
    child_copy.start()

    couple_copy.wait_recv()
    for k in range(parents):
        mine, other = c_ref[keep_box[k]], near_c[k]
        first = jnp.where(is_odd, other, mine)
        second = jnp.where(is_odd, mine, other)
        mixed_ref[k] = first + second.T
        child_ref[odd, k] = level_ref[keep_box[k]]

    child_copy.wait_recv()
    for k in range(parents):
        w_a = split(child_ref[0, k, K:])
        w_b = split(child_ref[1, k, K:])
        h = split(nn3(w_a, split(mixed_ref[k])))
        cross = nt3(h, tuple(rows(x, x) for x in w_b))
        turned = nt3(w_b, tuple(rows(x, x) for x in h))
        parent_ref[k, :K] = jnp.where(left, child_ref[0, k, :K], cross)
        parent_ref[k, K:] = jnp.where(left, turned, child_ref[1, k, :K])

    def write_two(k, z, w):
        out_two[0, 0, k] = z[:, :K]

    skeletonize(
        lambda k: parent_ref[k], lambda k: turn_ref[boxes + k],
        [count_two[0, 0, k] for k in range(parents)], write_two,
    )

    for part in range(2):
        for there, copy in copies(part):
            @pl.when(there)
            def _(copy=copy):
                copy.wait_send()
    couple_copy.wait_send()
    child_copy.wait_send()


def shards(sizes, *args):
    vmem = pl.BlockSpec(memory_space=pltpu.VMEM)
    smem = pl.BlockSpec(memory_space=pltpu.SMEM)
    anyw = pl.BlockSpec(memory_space=pl.ANY)
    return pl.pallas_call(
        functools.partial(kernel, sizes),
        out_shape=(
            jax.ShapeDtypeStruct((1, 1, 8, K, K), F32),
            jax.ShapeDtypeStruct((1, 1, 4, K, K), F32),
        ),
        in_specs=[anyw, anyw, anyw, vmem, smem, smem, vmem, smem],
        out_specs=(vmem, vmem),
        scratch_shapes=[
            pltpu.VMEM((8, M, M), F32),
            pltpu.VMEM((6, M, K), F32),
            pltpu.VMEM((8, M, M), F32),
            pltpu.VMEM((12, M, M), BF),
            pltpu.VMEM((2, 2 * K, M), F32),
            pltpu.VMEM((4, 2, 2 * K, M), F32),
            pltpu.VMEM((4, M, M), F32),
            pltpu.VMEM((4, M, M), F32),
            pltpu.VMEM((4, M, M), F32),
            pltpu.VMEM((4, 6 * K, 2 * M), F32),
            pltpu.VMEM((2, 4, M, M), F32),
            pltpu.VMEM((4, M, M), F32),
            pltpu.VMEM((8, M, M), F32),
            pltpu.VMEM((4, M, M), F32),
            pltpu.SemaphoreType.DMA((10,)),
            pltpu.SemaphoreType.DMA((10,)),
            pltpu.SemaphoreType.DMA((10,)),
        ],
        compiler_params=pltpu.CompilerParams(
            collective_id=0, has_side_effects=True, vmem_limit_bytes=32 << 20
        ),
        name="factor",
    )(*args)


def solution(mesh):
    return jax.shard_map(
        functools.partial(shards, (mesh.shape["gx"], mesh.shape["gy"])),
        mesh=mesh,
        in_specs=(
            P("gx", "gy", None, None, None),
            P(),
            P("gx", "gy", None, None, None),
            P("gx", "gy", None, None),
            P("gx", "gy", None),
            P("gx", "gy", None),
            P("gx", "gy", None, None),
            P("gx", "gy", None),
        ),
        out_specs=(P("gx", "gy", None, None, None), P("gx", "gy", None, None, None)),
        check_vma=False,
    )
```

profile of v0, /device:TPU:121, one launch (start us, length us, event | category | flops | bytes accessed | tf_op | source)
XLA Modules:
  0.0 36.6 jit_solution(4563974052121667077)
XLA Ops:
  0.6 0.0 copy-start.6
  0.6 0.0 copy-start.3
  0.7 0.0 copy-start.5
  0.7 0.0 copy-start.4
  0.7 0.0 copy-start.2
  0.7 0.0 copy-start
  0.7 1.2 %copy.10.faces_hbm = f32[6,128,64]{2,1,0:T(8,128)S(1)} copy(f32[6,128,64]{1,2,0:T(8,128)} %param.9) | data formatting | bytes 393216 | tf_op args[1]
  1.9 0.0 copy-done.6
  1.9 0.0 copy-done.3
  1.9 0.0 copy-done.5
  1.9 0.0 copy-done.4
  1.9 0.0 copy-done.2
  1.9 0.0 copy-done
  1.9 0.0 copy-start.1
  1.9 1.0 %copy-done.1 = f32[1,1,8,128,128]{4,3,2,1,0:T(8,128)S(1)} copy-done((f32[1,1,8,128,128]{4,3,2,1,0:T(8,128)S(1)}, f32[1,1,8,128,128]{4,3,2,1,0:T(8,128)}, u32[]{:S(2)}) %copy-start.1) | copy-done | bytes 524312
  3.0 32.2 %factor.1 = (f32[1,1,8,64,64]{4,3,2,1,0:T(8,128)S(1)}, f32[1,1,4,64,64]{4,3,2,1,0:T(8,128)S(1)}) custom-call(f32[1,1,8,128,128]{4,3,2,1,0:T(8,128)S(1)} %copy-done, f32[6,128,64]{2,1,0:T(8,128)S(1)} %copy.10.faces_hbm, f32[1,1,8,128,128]{4,3,2,1,0:T(8,128)S(1)} %copy-done.1, s32[1,1,8,128]{3,2,1,0:T(8,128)S(1)} %copy-done.2, s32[1,1,8]{2,1,0:T(1,128)S(1)} %copy-done.4, ...), custom_call_target="tpu_custom_call" | custom-call | tf_op jit(solution)/shard_map/factor/pallas_call | solution.py:346
  35.2 0.7 %copy.13 = f32[1,1,8,64,64]{4,3,2,1,0:T(8,128)} copy(f32[1,1,8,64,64]{4,3,2,1,0:T(8,128)S(1)} %get-tuple-element.4) | data formatting | bytes 262144
  35.9 0.7 %copy.14 = f32[1,1,4,64,64]{4,3,2,1,0:T(8,128)} copy(f32[1,1,4,64,64]{4,3,2,1,0:T(8,128)S(1)} %get-tuple-element.5) | data formatting | bytes 131072
Async XLA Ops:
  0.6 1.2 %copy-start.6 = (s32[1,1,4]{2,1,0:T(1,128)S(1)}, s32[1,1,4]{2,1,0:T(1,128)}, u32[]{:S(2)}) copy-start(s32[1,1,4]{2,1,0:T(1,128)} %count_two.1) | copy-start | bytes 52
  0.6 1.2 %copy-start.3 = (s32[1,1,4,128]{3,2,1,0:T(4,128)S(1)}, s32[1,1,4,128]{3,2,1,0:T(4,128)}, u32[]{:S(2)}) copy-start(s32[1,1,4,128]{3,2,1,0:T(4,128)} %order_two.1) | copy-start | bytes 6148
  0.7 1.2 %copy-start.5 = (s32[1,1,8]{2,1,0:T(1,128)S(1)}, s32[1,1,8]{2,1,0:T(1,128)}, u32[]{:S(2)}) copy-start(s32[1,1,8]{2,1,0:T(1,128)} %merge_map.1) | copy-start | bytes 100
  0.7 1.2 %copy-start.4 = (s32[1,1,8]{2,1,0:T(1,128)S(1)}, s32[1,1,8]{2,1,0:T(1,128)}, u32[]{:S(2)}) copy-start(s32[1,1,8]{2,1,0:T(1,128)} %count_one.1) | copy-start | bytes 100
  0.7 1.2 %copy-start.2 = (s32[1,1,8,128]{3,2,1,0:T(8,128)S(1)}, s32[1,1,8,128]{3,2,1,0:T(8,128)}, u32[]{:S(2)}) copy-start(s32[1,1,8,128]{3,2,1,0:T(8,128)} %order_one.1) | copy-start | bytes 12292
  0.7 1.2 %copy-start = (f32[1,1,8,128,128]{4,3,2,1,0:T(8,128)S(1)}, f32[1,1,8,128,128]{4,3,2,1,0:T(8,128)}, u32[]{:S(2)}) copy-start(f32[1,1,8,128,128]{4,3,2,1,0:T(8,128)} %blocks_hbm.1) | copy-start | bytes 1572868
  1.9 1.0 %copy-start.1 = (f32[1,1,8,128,128]{4,3,2,1,0:T(8,128)S(1)}, f32[1,1,8,128,128]{4,3,2,1,0:T(8,128)}, u32[]{:S(2)}) copy-start(f32[1,1,8,128,128]{4,3,2,1,0:T(8,128)} %couple_hbm.1) | copy-start | bytes 1572868
where the time goes:
time: 36.7 us; the launch traced here: 36.6 us
  Pallas kernels  32.2 us (88%)
  local copies, waits for them, and re-layouts  3.58 us (10%)
  between operations  0.75 us (2%)
    pallas_call x1, Pallas kernels, shards(): pl.pallas_call(functools.partial(kernel, sizes), out_shape=(jax.ShapeDtyp...  32.2 us
    unnamed x17, local copies, waits for them, and re-layouts  3.58 us

commit v1 on v0

--- a/solution.py
+++ b/solution.py
@@ -14,6 +14,7 @@
 NT = (((1,), (1,)), ((), ()))
 K = 64
 M = 128
+W = 32
 
 
 def dot(left, right, dims):
@@ -50,42 +51,64 @@
     return lax.broadcasted_iota(jnp.int32, shape, dim)
 
 
-def invert(pairs):
-    count = len(pairs)
-    left = iota((1, M), 1) < K
+def shifted(x, amount):
+    amount = amount % M
+    if amount == 0:
+        return x
+    return rows(x[M - amount :], x[: M - amount])
+
+
+def invert(groups):
+    n = len(groups)
+    lane = iota((1, M), 1)
     scales = []
-    tiles = [[] for _ in range(8)]
-    for n in pairs:
-        top = jnp.max(n, axis=0, keepdims=True)
-        first = jnp.max(jnp.where(left, top, 0.0), axis=1, keepdims=True)
-        second = jnp.max(jnp.where(left, 0.0, top), axis=1, keepdims=True)
-        scale = 1.0 / jnp.where(left, first, second)
-        scales.append(scale)
-        n = n * scale
-        for i in range(8):
-            tiles[i].append(n[8 * i : 8 * i + 8])
-    tiles = [jnp.stack(t) for t in tiles]
-    lane = iota((count, 8, M), 2)
-    half = jnp.where(lane >= K, K, 0)
-    within = iota((count, 1, M), 2) % K
-    sub = iota((count, 8, M), 1)
-
-    def body(t, tiles):
-        tiles = list(tiles)
+    for group in groups:
+        top = jnp.maximum(*[jnp.max(x, axis=0, keepdims=True) for x in group])
+        scale = jnp.ones((1, M), F32)
+        for s in range(M // W):
+            inside = lane // W == s
+            scale = jnp.where(
+                inside, jnp.max(jnp.where(inside, top, 0.0), axis=1, keepdims=True), scale
+            )
+        scales.append(1.0 / scale)
+    tiles = [
+        [jnp.stack([g[j][8 * i : 8 * i + 8] * sc for g, sc in zip(groups, scales)]) for j in range(2)]
+        for i in range(8)
+    ]
+    sub = iota((n, 8, M), 1)
+    within = iota((n, 8, M), 2) % W
+    segment = iota((8 * n, 8, M), 2) // W * W
+    for t in range(8):
+        here, first = divmod(8 * t, W)
+        source = jnp.concatenate([tiles[i][here] for i in range(8)], axis=0)
+        cols = []
         for q in range(8):
-            step = t * 8 + q
-            place = half + step
-            cols = [jnp.take_along_axis(x, place, axis=2, mode="promise_in_bounds") for x in tiles]
-            row = tiles[0][:, q : q + 1, :]
-            inverse = 1.0 / cols[0][:, q : q + 1, :]
-            row = jnp.where(within == step, 1.0 + inverse, row * inverse)
-            cols[0] = jnp.where(sub == q, cols[0] - 1.0, cols[0])
-            tiles = [x - c * row for x, c in zip(tiles, cols)]
-        return tuple(tiles[1:] + tiles[:1])
-
-    tiles = lax.fori_loop(0, 8, body, tuple(tiles))
+            got = jnp.take_along_axis(source, segment + (first + q), axis=2, mode="promise_in_bounds")
+            cols.append([got[n * i : n * i + n] for i in range(8)])
+        unit = within == sub + first
+        x = list(tiles[t])
+        x[here] = jnp.where(
+            (within >= first) & (within < first + 8), jnp.where(unit, 1.0, 0.0), x[here]
+        )
+        c = [cols[q][t] for q in range(8)]
+        for k in range(8):
+            inverse = 1.0 / c[k][:, k : k + 1, :]
+            factor = jnp.where(sub == k, c[k] - 1.0, c[k])
+            for q in range(k + 1, 8):
+                c[q] = c[q] - factor * (c[q][:, k : k + 1, :] * inverse)
+            x = [v - factor * (v[:, k : k + 1, :] * inverse) for v in x]
+        r = list(x)
+        r[here] = jnp.where(unit, x[here] + 1.0, x[here])
+        for i in [(t + 1 + step) % 8 for step in range(7)]:
+            for j in range(2):
+                terms = [cols[q][i] * r[j][:, q : q + 1, :] for q in range(8)]
+                while len(terms) > 1:
+                    terms = [one + two for one, two in zip(terms[::2], terms[1::2])]
+                tiles[i][j] = tiles[i][j] - terms[0]
+        tiles[t] = x
     return [
-        rows(*[tiles[i][p] for i in range(8)]) * scales[p] for p in range(count)
+        [jnp.concatenate([tiles[i][j][p] for i in range(8)], axis=0) * scales[p] for j in range(2)]
+        for p in range(n)
     ]
 
 
@@ -93,55 +116,74 @@
     boxes = len(counts)
     row_of = iota((K, M), 0)
     lane_of = iota((K, M), 1)
-    left = lane_of < K
-    diagonal = (lane_of % K) == row_of
-    normals, sides = [], []
-    for b in range(0, boxes, 2):
-        halves = []
-        for i in (0, 1):
-            c = counts[b + i]
-            ah, al = split(read_block(b + i))
-            turn = turn_of(b + i)
+    inner = lane_of % W
+    segment = lane_of // W
+    natural = [(lane_of + (M - W * r)) % M for r in range(4)]
+    groups, sides = [], []
+    for g in range(0, boxes, 4):
+        grams = []
+        for r in range(4):
+            ah, al = split(read_block(g + r))
+            turn = turn_of(g + r)
             turned = split(dot(lanes(turn, turn), lanes(ah, al), NT))
-            skel = tuple(jnp.where(row_of < c, x[:K], jnp.zeros_like(x[:K])) for x in turned)
-            gram = nt3(skel, turned)
-            sides.append(jnp.where(lane_of >= c, gram, 0.0))
-            normal = jnp.where(lane_of < c, gram, 0.0)
-            if i == 1:
-                normal = pltpu.roll(normal, K, 1)
-                c_here = counts[b + 1]
-            halves.append(normal)
-        padded = jnp.where(row_of >= jnp.where(left, counts[b], counts[b + 1]), 1.0, 0.0)
-        normals.append(
-            jnp.where(left, halves[0], halves[1]) + jnp.where(diagonal, padded, 0.0)
+            skel = tuple(
+                jnp.where(row_of < counts[g + r], y, jnp.zeros_like(y))
+                for y in (shifted(x, -W * r)[:K] for x in turned)
+            )
+            gram = nt3(skel, tuple(rows(x, shifted(x, -W)) for x in turned))
+            sides.append(jnp.where(natural[r] >= counts[g + r], gram[:, :M], 0.0))
+            grams.append(gram)
+        count = jnp.where(
+            segment < 2,
+            jnp.where(segment == 0, counts[g], counts[g + 1]),
+            jnp.where(segment == 2, counts[g + 2], counts[g + 3]),
         )
-    inverses = invert(normals)
-    for b in range(0, boxes, 2):
-        zero = jnp.zeros((K, M), BF)
-        firsts, seconds = split(sides[b]), split(sides[b + 1])
+        group = []
+        for j in range(2):
+            parts = [x[:, M * j : M * j + M] for x in grams]
+            normal = jnp.where(
+                segment < 2,
+                jnp.where(segment == 0, parts[0], parts[1]),
+                jnp.where(segment == 2, parts[2], parts[3]),
+            )
+            column = inner + W * j
+            normal = jnp.where(column < count, normal, 0.0)
+            group.append(normal + jnp.where((column == row_of) & (row_of >= count), 1.0, 0.0))
+        groups.append(group)
+    inverses = invert(groups)
+    for g in range(0, boxes, 4):
+        inverse = split(lanes(*inverses[g // 4]))
+        seg = iota((K, 2 * M), 1) % M // W
+        stacked = tuple(
+            rows(*[jnp.where(seg == r, x, jnp.zeros_like(x)) for r in range(4)]) for x in inverse
+        )
+        right = [split(sides[g + r]) for r in range(4)]
         right = tuple(
-            rows(lanes(f, zero), lanes(zero, s)) for f, s in zip(firsts, seconds)
+            rows(*[right[r][h][W * j : W * j + W] for j in range(2) for r in range(4)])
+            for h in range(2)
         )
-        interp = nn3(split(inverses[b // 2]), right)
-        for i in (0, 1):
-            c = counts[b + i]
-            keep = jnp.where((lane_of == row_of) & (row_of < c), 1.0, 0.0)
-            short = split(interp[:, M * i : M * i + M] + keep)
-            turn = turn_of(b + i)
+        interp = nn3(stacked, right)
+        for r in range(4):
+            b = g + r
+            c = counts[b]
+            keep = jnp.where((natural[r] == row_of) & (row_of < c), 1.0, 0.0)
+            short = split(interp[K * r : K * r + K] + keep)
+            turn = turn_of(b)
             weights = dot(lanes(*short), rows(turn, turn), NN)
             parts = split(weights)
-            applied = split(nn3(parts, split(read_block(b + i))))
+            applied = split(nn3(parts, split(read_block(b))))
             twice = tuple(rows(x, x) for x in parts)
-            pad = jnp.where(diagonal & (row_of >= c), 1.0, 0.0)
-            write(b + i, nt3(applied, twice) + pad, weights)
+            pad = jnp.where((lane_of % K == row_of) & (row_of >= c), 1.0, 0.0)
+            write(b, nt3(applied, twice) + pad, weights)
 
 
 def kernel(
     sizes,
-    blocks_hbm, faces_hbm, couple_hbm, order_one, count_one, merge_map, order_two, count_two,
+    blocks_hbm, faces_hbm, couple_hbm, small_a, small_b, small_c, small_d, small_e,
     out_one, out_two,
     a_ref, face_ref, c_ref, turn_ref, own_ref, near_ref, send_c, near_c, mixed_ref,
     q_ref, child_ref, send_child, level_ref, parent_ref,
+    order_one, order_two, count_one, count_two, merge_map,
     load_sems, send_sems, recv_sems,
 ):
     nx, ny = sizes
@@ -153,7 +195,16 @@
     loads = [pltpu.make_async_copy(blocks_hbm.at[0, 0, b], a_ref.at[b], load_sems.at[b]) for b in range(boxes)]
     load_face = pltpu.make_async_copy(faces_hbm, face_ref, load_sems.at[8])
     load_c = pltpu.make_async_copy(couple_hbm.at[0, 0], c_ref, load_sems.at[9])
-    for load in loads:
+    small_loads = [
+        pltpu.make_async_copy(source, target, load_sems.at[10 + i])
+        for i, (source, target) in enumerate(
+            zip(
+                (small_a, small_b, small_c, small_d, small_e),
+                (order_one, count_one, merge_map, order_two, count_two),
+            )
+        )
+    ]
+    for load in small_loads + loads:
         load.start()
     load_face.start()
     load_c.start()
@@ -171,12 +222,14 @@
         def _(where=where):
             pl.semaphore_signal(barrier, inc=1, device_id=where, device_id_type=MESH)
 
+    for load in small_loads:
+        load.wait()
     orders = rows(
         order_one[0, 0].astype(F32), order_two[0, 0].astype(F32), jnp.zeros((4, M), F32)
     ).T
     lane = iota((M, M), 1).astype(F32)
     for b in range(boxes + parents):
-        turn_ref[b] = jnp.where(orders[:, b : b + 1] == lane, 1.0, 0.0).astype(BF)
+        turn_ref[b] = shifted(jnp.where(orders[:, b : b + 1] == lane, 1.0, 0.0).astype(BF), W * (b % 4))
 
     row_of = iota((K, M), 0)
     lane_of = iota((K, M), 1)
@@ -201,7 +254,7 @@
             halves = []
             for i in (0, 1):
                 loads[b + i].wait()
-                turn = turn_ref[b + i]
+                turn = shifted(turn_ref[b + i], -W * ((b + i) % 4))
                 ah, al = split(a_ref[b + i])
                 picked = split(dot(lanes(turn[:K], turn[:K]), rows(ah, al), NN))
                 other = turn if i == 0 else rows(turn[K:], turn[:K])
@@ -248,12 +301,21 @@
 
     load_face.wait()
 
+    def mix_couples():
+        couple_copy.wait_recv()
+        for k in range(parents):
+            mine, other = c_ref[keep_box[k]], near_c[k]
+            first = jnp.where(is_odd, other, mine)
+            second = jnp.where(is_odd, mine, other)
+            mixed_ref[k] = first + second.T
+
     def project(f, source):
         face = split(face_ref[f])
-        zero = jnp.zeros((M, K), BF)
+        zero = jnp.zeros((K, M), BF)
         right = tuple(rows(lanes(x, zero), lanes(zero, x)) for x in face)
-        return nt3(split(source), right)
-
+        return nn3(split(source), right)
+
+    all_faces = split(face_ref[...].reshape(6 * K, M).T)
     for f in (4, 5):
         q = project(f, own_ref[...].reshape(4 * K, M))
         for b in range(boxes):
@@ -267,6 +329,8 @@
         q_ref[edge // 2, f * K : f * K + K, M * (edge % 2) : M * (edge % 2) + M] = jnp.zeros((K, M), F32)
 
     for f in range(4):
+        if f == 2:
+            mix_couples()
         there = sides[f][0]
         for part in range(2):
             @pl.when(there)
@@ -283,7 +347,6 @@
         for p in range(4):
             q_ref[p, f * K : f * K + K, :] = q[p * K : p * K + K]
 
-    all_faces = split(lanes(*[face_ref[f] for f in range(6)]))
     for p in range(4):
         d = nn3(all_faces, split(q_ref[p]))
         for i in (0, 1):
@@ -304,12 +367,7 @@
     )
     child_copy.start()
 
-    couple_copy.wait_recv()
     for k in range(parents):
-        mine, other = c_ref[keep_box[k]], near_c[k]
-        first = jnp.where(is_odd, other, mine)
-        second = jnp.where(is_odd, mine, other)
-        mixed_ref[k] = first + second.T
         child_ref[odd, k] = level_ref[keep_box[k]]
 
     child_copy.wait_recv()
@@ -339,21 +397,20 @@
     child_copy.wait_send()
 
 
-def shards(sizes, *args):
+def shards(sizes, blocks, face_maps, *others):
     vmem = pl.BlockSpec(memory_space=pltpu.VMEM)
-    smem = pl.BlockSpec(memory_space=pltpu.SMEM)
-    anyw = pl.BlockSpec(memory_space=pl.ANY)
+    hbm = pl.BlockSpec(memory_space=pltpu.HBM)
     return pl.pallas_call(
         functools.partial(kernel, sizes),
         out_shape=(
             jax.ShapeDtypeStruct((1, 1, 8, K, K), F32),
             jax.ShapeDtypeStruct((1, 1, 4, K, K), F32),
         ),
-        in_specs=[anyw, anyw, anyw, vmem, smem, smem, vmem, smem],
+        in_specs=[hbm] * 8,
         out_specs=(vmem, vmem),
         scratch_shapes=[
             pltpu.VMEM((8, M, M), F32),
-            pltpu.VMEM((6, M, K), F32),
+            pltpu.VMEM((6, K, M), F32),
             pltpu.VMEM((8, M, M), F32),
             pltpu.VMEM((12, M, M), BF),
             pltpu.VMEM((2, 2 * K, M), F32),
@@ -366,15 +423,20 @@
             pltpu.VMEM((4, M, M), F32),
             pltpu.VMEM((8, M, M), F32),
             pltpu.VMEM((4, M, M), F32),
-            pltpu.SemaphoreType.DMA((10,)),
+            pltpu.VMEM((1, 1, 8, M), jnp.int32),
+            pltpu.VMEM((1, 1, 4, M), jnp.int32),
+            pltpu.SMEM((1, 1, 8), jnp.int32),
+            pltpu.SMEM((1, 1, 4), jnp.int32),
+            pltpu.SMEM((1, 1, 8), jnp.int32),
+            pltpu.SemaphoreType.DMA((15,)),
             pltpu.SemaphoreType.DMA((10,)),
             pltpu.SemaphoreType.DMA((10,)),
         ],
         compiler_params=pltpu.CompilerParams(
-            collective_id=0, has_side_effects=True, vmem_limit_bytes=32 << 20
+            collective_id=0, has_side_effects=True, vmem_limit_bytes=56 << 20
         ),
         name="factor",
-    )(*args)
+    )(blocks, jnp.swapaxes(face_maps, 1, 2), *others)
 
 
 def solution(mesh):

time: 36.7 us -> 29 us (0.79)
  Pallas kernels: 32.2 us -> 25.9 us
  local copies, waits for them, and re-layouts: 3.58 us -> 2.37 us
    pallas_call x1, Pallas kernels: 32.2 us -> 25.9 us  [shards(): pl.pallas_call(functools.partial(kernel, sizes), out_shape=(jax.ShapeDtyp...]
    unnamed x17 -> x4, local copies, waits for them, and re-layouts: 3.58 us -> 2.37 us
where the time goes in v1:
time: 29 us; the launch traced here: 28.9 us
  Pallas kernels  25.9 us (89%)
  local copies, waits for them, and re-layouts  2.37 us (8%)
  between operations  0.65 us (2%)
    pallas_call x1, Pallas kernels, shards(): pl.pallas_call(functools.partial(kernel, sizes), out_shape=(jax.ShapeDtyp...  25.9 us
    unnamed x4, local copies, waits for them, and re-layouts  2.37 us

profile of v1, /device:TPU:121, one launch (start us, length us, event | category | flops | bytes accessed | tf_op | source)
XLA Modules:
  0.0 28.9 jit_solution(10441111160773412951)
XLA Ops:
  0.6 25.9 %factor.1 = (f32[1,1,8,64,64]{4,3,2,1,0:T(8,128)}, f32[1,1,4,64,64]{4,3,2,1,0:T(8,128)}) custom-call(f32[1,1,8,128,128]{4,3,2,1,0:T(8,128)} %blocks_hbm.1, f32[6,64,128]{2,1,0:T(8,128)} %bitcast.1, f32[1,1,8,128,128]{4,3,2,1,0:T(8,128)} %couple_hbm.1, s32[1,1,8,128]{3,2,1,0:T(8,128)} %small_a.1, s32[1,1,8]{2,1,0:T(1,128)} %small_b.1, s32[1,1,8]{2,1,0:T(1,128)} %small_c.1, ...), custom_call_target="tpu_custom_call" | custom-call | tf_op jit(solution)/shard_map/factor/pallas_call | solution.py:403
  26.5 0.0 copy-start
  26.5 1.7 %copy.12 = f32[1,1,8,64,64]{4,3,2,1,0:T(8,128)} copy(f32[1,1,8,64,64]{4,3,2,1,0:T(8,128)} %get-tuple-element.4) | data formatting | bytes 262144
  28.2 0.0 copy-done
  28.2 0.7 %copy.13 = f32[1,1,4,64,64]{4,3,2,1,0:T(8,128)} copy(f32[1,1,4,64,64]{4,3,2,1,0:T(8,128)S(1)} %copy-done) | data formatting | bytes 131072
Async XLA Ops:
  26.5 1.7 %copy-start = (f32[1,1,4,64,64]{4,3,2,1,0:T(8,128)S(1)}, f32[1,1,4,64,64]{4,3,2,1,0:T(8,128)}, u32[]{:S(2)}) copy-start(f32[1,1,4,64,64]{4,3,2,1,0:T(8,128)} %get-tuple-element.5) | copy-start | bytes 196612

commit v2 on v1

--- a/solution.py
+++ b/solution.py
@@ -112,26 +112,26 @@
     ]
 
 
-def skeletonize(read_block, turn_of, counts, write):
+def skeletonize(read_block, turn_of, counts, write, weigh=None, between=None):
     boxes = len(counts)
     row_of = iota((K, M), 0)
     lane_of = iota((K, M), 1)
     inner = lane_of % W
     segment = lane_of // W
     natural = [(lane_of + (M - W * r)) % M for r in range(4)]
-    groups, sides = [], []
+    groups, sides, centres = [], [], []
     for g in range(0, boxes, 4):
         grams = []
         for r in range(4):
             ah, al = split(read_block(g + r))
             turn = turn_of(g + r)
             turned = split(dot(lanes(turn, turn), lanes(ah, al), NT))
-            skel = tuple(
-                jnp.where(row_of < counts[g + r], y, jnp.zeros_like(y))
-                for y in (shifted(x, -W * r)[:K] for x in turned)
-            )
+            skel = tuple(shifted(x, -W * r)[:K] for x in turned)
             gram = nt3(skel, tuple(rows(x, shifted(x, -W)) for x in turned))
-            sides.append(jnp.where(natural[r] >= counts[g + r], gram[:, :M], 0.0))
+            if weigh is None:
+                centres.append(dot(lanes(turn, turn), lanes(*turned), NT))
+            live = (natural[r] >= counts[g + r]) & (row_of < counts[g + r])
+            sides.append(split(jnp.where(live, gram[:, :M], 0.0)))
             grams.append(gram)
         count = jnp.where(
             segment < 2,
@@ -147,34 +147,42 @@
                 jnp.where(segment == 2, parts[2], parts[3]),
             )
             column = inner + W * j
-            normal = jnp.where(column < count, normal, 0.0)
+            normal = jnp.where((column < count) & (row_of < count), normal, 0.0)
             group.append(normal + jnp.where((column == row_of) & (row_of >= count), 1.0, 0.0))
         groups.append(group)
     inverses = invert(groups)
+    shorts, parts = [], []
+    chosen = iota((1, 2 * M), 1) % M // W
     for g in range(0, boxes, 4):
         inverse = split(lanes(*inverses[g // 4]))
-        seg = iota((K, 2 * M), 1) % M // W
         stacked = tuple(
-            rows(*[jnp.where(seg == r, x, jnp.zeros_like(x)) for r in range(4)]) for x in inverse
-        )
-        right = [split(sides[g + r]) for r in range(4)]
+            rows(*[x * jnp.where(chosen == r, 1.0, 0.0).astype(BF) for r in range(4)])
+            for x in inverse
+        )
         right = tuple(
-            rows(*[right[r][h][W * j : W * j + W] for j in range(2) for r in range(4)])
+            rows(*[sides[g + r][h][W * j : W * j + W] for j in range(2) for r in range(4)])
             for h in range(2)
         )
         interp = nn3(stacked, right)
         for r in range(4):
-            b = g + r
-            c = counts[b]
-            keep = jnp.where((natural[r] == row_of) & (row_of < c), 1.0, 0.0)
-            short = split(interp[K * r : K * r + K] + keep)
+            keep = jnp.where((natural[r] == row_of) & (row_of < counts[g + r]), 1.0, 0.0)
+            shorts.append(split(interp[K * r : K * r + K] + keep))
+    if weigh is not None:
+        for b in range(boxes):
             turn = turn_of(b)
-            weights = dot(lanes(*short), rows(turn, turn), NN)
-            parts = split(weights)
-            applied = split(nn3(parts, split(read_block(b))))
-            twice = tuple(rows(x, x) for x in parts)
-            pad = jnp.where((lane_of % K == row_of) & (row_of >= c), 1.0, 0.0)
-            write(b, nt3(applied, twice) + pad, weights)
+            weights = dot(lanes(*shorts[b]), rows(turn, turn), NN)
+            weigh(b, weights)
+            parts.append(split(weights))
+        between()
+    for b in range(boxes):
+        if weigh is None:
+            left, middle = shorts[b], centres[b]
+        else:
+            left, middle = parts[b], read_block(b)
+        applied = split(nn3(left, split(middle)))
+        twice = tuple(rows(x, x) for x in left)
+        pad = jnp.where((lane_of % K == row_of) & (row_of >= counts[b]), 1.0, 0.0)
+        write(b, nt3(applied, twice) + pad)
 
 
 def kernel(
@@ -182,7 +190,7 @@
     blocks_hbm, faces_hbm, couple_hbm, small_a, small_b, small_c, small_d, small_e,
     out_one, out_two,
     a_ref, face_ref, c_ref, turn_ref, own_ref, near_ref, send_c, near_c, mixed_ref,
-    q_ref, child_ref, send_child, level_ref, parent_ref,
+    q_ref, child_w, child_z, send_w, send_z, level_w, level_z, cross_ref, parent_ref,
     order_one, order_two, count_one, count_two, merge_map,
     load_sems, send_sems, recv_sems,
 ):
@@ -228,8 +236,12 @@
         order_one[0, 0].astype(F32), order_two[0, 0].astype(F32), jnp.zeros((4, M), F32)
     ).T
     lane = iota((M, M), 1).astype(F32)
-    for b in range(boxes + parents):
+
+    def build_turn(b):
         turn_ref[b] = shifted(jnp.where(orders[:, b : b + 1] == lane, 1.0, 0.0).astype(BF), W * (b % 4))
+
+    for b in range(boxes):
+        build_turn(b)
 
     row_of = iota((K, M), 0)
     lane_of = iota((K, M), 1)
@@ -294,6 +306,9 @@
     )
     couple_copy.start()
 
+    for k in range(parents):
+        build_turn(boxes + k)
+
     for there, _, face in sides:
         @pl.when(jnp.logical_not(there))
         def _(face=face):
@@ -352,35 +367,52 @@
         for i in (0, 1):
             a_ref[2 * p + i] = a_ref[2 * p + i] - d[:, M * i : M * i + M]
 
-    def write_one(b, z, w):
-        level_ref[b, :K] = z
-        level_ref[b, K:] = w
+    def child_copy(i, source, target):
+        return pltpu.make_async_remote_copy(
+            src_ref=source, dst_ref=target.at[odd], send_sem=send_sems.at[9 + i],
+            recv_sem=recv_sems.at[9 + i], device_id=partner, device_id_type=MESH,
+        )
+
+    w_copy = child_copy(0, send_w, child_w)
+    z_copy = child_copy(1, send_z, child_z)
+
+    def weigh(b, w):
+        level_w[b] = w
+
+    def send_weights():
+        for k in range(parents):
+            send_w[k] = level_w[send_box[k]]
+        w_copy.start()
+        for k in range(parents):
+            child_w[odd, k] = level_w[keep_box[k]]
+
+    def write_one(b, z):
+        level_z[b] = z
         out_one[0, 0, b] = z[:, :K]
 
-    skeletonize(lambda b: a_ref[b], lambda b: turn_ref[b], counts, write_one)
-
-    for k in range(parents):
-        send_child[k] = level_ref[send_box[k]]
-    child_copy = pltpu.make_async_remote_copy(
-        src_ref=send_child, dst_ref=child_ref.at[odd], send_sem=send_sems.at[9],
-        recv_sem=recv_sems.at[9], device_id=partner, device_id_type=MESH,
+    skeletonize(
+        lambda b: a_ref[b], lambda b: turn_ref[b], counts, write_one, weigh, send_weights
     )
-    child_copy.start()
-
-    for k in range(parents):
-        child_ref[odd, k] = level_ref[keep_box[k]]
-
-    child_copy.wait_recv()
-    for k in range(parents):
-        w_a = split(child_ref[0, k, K:])
-        w_b = split(child_ref[1, k, K:])
+
+    for k in range(parents):
+        send_z[k] = level_z[send_box[k]]
+    z_copy.start()
+    for k in range(parents):
+        child_z[odd, k] = level_z[keep_box[k]]
+
+    w_copy.wait_recv()
+    for k in range(parents):
+        w_a = split(child_w[0, k])
+        w_b = split(child_w[1, k])
         h = split(nn3(w_a, split(mixed_ref[k])))
-        cross = nt3(h, tuple(rows(x, x) for x in w_b))
-        turned = nt3(w_b, tuple(rows(x, x) for x in h))
-        parent_ref[k, :K] = jnp.where(left, child_ref[0, k, :K], cross)
-        parent_ref[k, K:] = jnp.where(left, turned, child_ref[1, k, :K])
-
-    def write_two(k, z, w):
+        cross_ref[0, k] = nt3(h, tuple(rows(x, x) for x in w_b))
+        cross_ref[1, k] = nt3(w_b, tuple(rows(x, x) for x in h))
+    z_copy.wait_recv()
+    for k in range(parents):
+        parent_ref[k, :K] = jnp.where(left, child_z[0, k], cross_ref[0, k])
+        parent_ref[k, K:] = jnp.where(left, cross_ref[1, k], child_z[1, k])
+
+    def write_two(k, z):
         out_two[0, 0, k] = z[:, :K]
 
     skeletonize(
@@ -394,7 +426,8 @@
             def _(copy=copy):
                 copy.wait_send()
     couple_copy.wait_send()
-    child_copy.wait_send()
+    w_copy.wait_send()
+    z_copy.wait_send()
 
 
 def shards(sizes, blocks, face_maps, *others):
@@ -419,9 +452,13 @@
             pltpu.VMEM((4, M, M), F32),
             pltpu.VMEM((4, M, M), F32),
             pltpu.VMEM((4, 6 * K, 2 * M), F32),
-            pltpu.VMEM((2, 4, M, M), F32),
-            pltpu.VMEM((4, M, M), F32),
-            pltpu.VMEM((8, M, M), F32),
+            pltpu.VMEM((2, 4, K, M), F32),
+            pltpu.VMEM((2, 4, K, M), F32),
+            pltpu.VMEM((4, K, M), F32),
+            pltpu.VMEM((4, K, M), F32),
+            pltpu.VMEM((8, K, M), F32),
+            pltpu.VMEM((8, K, M), F32),
+            pltpu.VMEM((2, 4, K, M), F32),
             pltpu.VMEM((4, M, M), F32),
             pltpu.VMEM((1, 1, 8, M), jnp.int32),
             pltpu.VMEM((1, 1, 4, M), jnp.int32),
@@ -429,8 +466,8 @@
             pltpu.SMEM((1, 1, 4), jnp.int32),
             pltpu.SMEM((1, 1, 8), jnp.int32),
             pltpu.SemaphoreType.DMA((15,)),
-            pltpu.SemaphoreType.DMA((10,)),
-            pltpu.SemaphoreType.DMA((10,)),
+            pltpu.SemaphoreType.DMA((11,)),
+            pltpu.SemaphoreType.DMA((11,)),
         ],
         compiler_params=pltpu.CompilerParams(
             collective_id=0, has_side_effects=True, vmem_limit_bytes=56 << 20

time: 29 us -> 25.8 us (0.89)
  Pallas kernels: 25.9 us -> 22.7 us
    pallas_call x1, Pallas kernels: 25.9 us -> 22.7 us  [shards(): pl.pallas_call(functools.partial(kernel, sizes), out_shape=(jax.ShapeDtyp...]
where the time goes in v2:
time: 25.8 us; the launch traced here: 25.7 us
  Pallas kernels  22.7 us (88%)
  local copies, waits for them, and re-layouts  2.37 us (9%)
  between operations  0.65 us (3%)
    pallas_call x1, Pallas kernels, shards(): pl.pallas_call(functools.partial(kernel, sizes), out_shape=(jax.ShapeDtyp...  22.7 us
    unnamed x4, local copies, waits for them, and re-layouts  2.37 us

profile of v2, /device:TPU:121, one launch (start us, length us, event | category | flops | bytes accessed | tf_op | source)
XLA Modules:
  0.0 25.7 jit_solution(1866336725335136944)
XLA Ops:
  0.6 22.7 %factor.1 = (f32[1,1,8,64,64]{4,3,2,1,0:T(8,128)}, f32[1,1,4,64,64]{4,3,2,1,0:T(8,128)}) custom-call(f32[1,1,8,128,128]{4,3,2,1,0:T(8,128)} %blocks_hbm.1, f32[6,64,128]{2,1,0:T(8,128)} %bitcast.1, f32[1,1,8,128,128]{4,3,2,1,0:T(8,128)} %couple_hbm.1, s32[1,1,8,128]{3,2,1,0:T(8,128)} %small_a.1, s32[1,1,8]{2,1,0:T(1,128)} %small_b.1, s32[1,1,8]{2,1,0:T(1,128)} %small_c.1, ...), custom_call_target="tpu_custom_call" | custom-call | tf_op jit(solution)/shard_map/factor/pallas_call | solution.py:436
  23.3 0.0 copy-start
  23.3 1.7 %copy.12 = f32[1,1,8,64,64]{4,3,2,1,0:T(8,128)} copy(f32[1,1,8,64,64]{4,3,2,1,0:T(8,128)} %get-tuple-element.4) | data formatting | bytes 262144
  25.0 0.0 copy-done
  25.0 0.7 %copy.13 = f32[1,1,4,64,64]{4,3,2,1,0:T(8,128)} copy(f32[1,1,4,64,64]{4,3,2,1,0:T(8,128)S(1)} %copy-done) | data formatting | bytes 131072
Async XLA Ops:
  23.3 1.7 %copy-start = (f32[1,1,4,64,64]{4,3,2,1,0:T(8,128)S(1)}, f32[1,1,4,64,64]{4,3,2,1,0:T(8,128)}, u32[]{:S(2)}) copy-start(f32[1,1,4,64,64]{4,3,2,1,0:T(8,128)} %get-tuple-element.5) | copy-start | bytes 196612

commit v3 on v2

--- a/solution.py
+++ b/solution.py
@@ -77,34 +77,49 @@
     ]
     sub = iota((n, 8, M), 1)
     within = iota((n, 8, M), 2) % W
-    segment = iota((8 * n, 8, M), 2) // W * W
+    segment = iota((1, 8, M), 2) // W * W
+
+    def spread(parts, lane_at):
+        source = jnp.concatenate(parts, axis=0)
+        place = jnp.broadcast_to(segment + lane_at, source.shape)
+        got = jnp.take_along_axis(source, place, axis=2, mode="promise_in_bounds")
+        return [got[n * i : n * i + n] for i in range(len(parts))]
+
+    def update(value, factors, row):
+        terms = [f * row[:, q : q + 1, :] for q, f in enumerate(factors)]
+        while len(terms) > 1:
+            terms = [one + two for one, two in zip(terms[::2], terms[1::2])]
+        return value - terms[0]
+
+    c = [spread([tiles[0][0], tiles[1][0]], q)[0] for q in range(8)]
     for t in range(8):
         here, first = divmod(8 * t, W)
-        source = jnp.concatenate([tiles[i][here] for i in range(8)], axis=0)
-        cols = []
-        for q in range(8):
-            got = jnp.take_along_axis(source, segment + (first + q), axis=2, mode="promise_in_bounds")
-            cols.append([got[n * i : n * i + n] for i in range(8)])
+        after, start = divmod(8 * t + 8, W)
+        ahead = [
+            spread([tiles[t][after], tiles[t + 1][after]], start + q) for q in range(8)
+        ] if t < 7 else []
+        others = [(t + 1 + step) % 8 for step in range(7)]
+        cols = [spread([tiles[i][here] for i in others], first + q) for q in range(8)]
         unit = within == sub + first
         x = list(tiles[t])
         x[here] = jnp.where(
             (within >= first) & (within < first + 8), jnp.where(unit, 1.0, 0.0), x[here]
         )
-        c = [cols[q][t] for q in range(8)]
+        same = [pair[0] for pair in ahead]
         for k in range(8):
             inverse = 1.0 / c[k][:, k : k + 1, :]
             factor = jnp.where(sub == k, c[k] - 1.0, c[k])
             for q in range(k + 1, 8):
                 c[q] = c[q] - factor * (c[q][:, k : k + 1, :] * inverse)
             x = [v - factor * (v[:, k : k + 1, :] * inverse) for v in x]
+            same = [v - factor * (v[:, k : k + 1, :] * inverse) for v in same]
+        beside = [cols[q][0] for q in range(8)]
+        c = [update(pair[1], beside, v) for pair, v in zip(ahead, same)]
         r = list(x)
         r[here] = jnp.where(unit, x[here] + 1.0, x[here])
-        for i in [(t + 1 + step) % 8 for step in range(7)]:
+        for m, i in enumerate(others):
             for j in range(2):
-                terms = [cols[q][i] * r[j][:, q : q + 1, :] for q in range(8)]
-                while len(terms) > 1:
-                    terms = [one + two for one, two in zip(terms[::2], terms[1::2])]
-                tiles[i][j] = tiles[i][j] - terms[0]
+                tiles[i][j] = update(tiles[i][j], [cols[q][m] for q in range(8)], r[j])
         tiles[t] = x
     return [
         [jnp.concatenate([tiles[i][j][p] for i in range(8)], axis=0) * scales[p] for j in range(2)]
@@ -254,27 +269,26 @@
             got.append((there, pltpu.make_async_remote_copy(
                 src_ref=own_ref.at[part],
                 dst_ref=near_ref.at[face, part],
-                send_sem=send_sems.at[2 * d + part],
-                recv_sem=recv_sems.at[2 * face + part],
+                send_sem=send_sems.at[4 * d + part],
+                recv_sem=recv_sems.at[4 * face + part],
                 device_id=where,
                 device_id_type=MESH,
             )))
         return got
 
-    for part in range(2):
-        for b in range(4 * part, 4 * part + 4, 2):
-            halves = []
-            for i in (0, 1):
-                loads[b + i].wait()
-                turn = shifted(turn_ref[b + i], -W * ((b + i) % 4))
-                ah, al = split(a_ref[b + i])
-                picked = split(dot(lanes(turn[:K], turn[:K]), rows(ah, al), NN))
-                other = turn if i == 0 else rows(turn[K:], turn[:K])
-                halves.append(dot(lanes(*picked), lanes(other, other), NT))
-            c = jnp.where(left, counts[b], counts[b + 1])
-            s = jnp.where(left, halves[0], halves[1])
-            s = jnp.where((row_of < c) & (lane_of % K < c), s, 0.0)
-            own_ref[part, (b % 4) // 2 * K : (b % 4) // 2 * K + K, :] = s
+    for part in range(4):
+        halves = []
+        for i in (0, 1):
+            b = 2 * part + i
+            loads[b].wait()
+            turn = shifted(turn_ref[b], -W * (b % 4))
+            ah, al = split(a_ref[b])
+            picked = split(dot(lanes(turn[:K], turn[:K]), rows(ah, al), NN))
+            other = turn if i == 0 else rows(turn[K:], turn[:K])
+            halves.append(dot(lanes(*picked), lanes(other, other), NT))
+        c = jnp.where(left, counts[2 * part], counts[2 * part + 1])
+        s = jnp.where(left, halves[0], halves[1])
+        own_ref[part] = jnp.where((row_of < c) & (lane_of % K < c), s, 0.0)
         if part == 0:
             pl.semaphore_wait(
                 barrier,
@@ -301,7 +315,7 @@
     for k in range(parents):
         send_c[k] = c_ref[send_box[k]]
     couple_copy = pltpu.make_async_remote_copy(
-        src_ref=send_c, dst_ref=near_c, send_sem=send_sems.at[8], recv_sem=recv_sems.at[8],
+        src_ref=send_c, dst_ref=near_c, send_sem=send_sems.at[16], recv_sem=recv_sems.at[16],
         device_id=partner, device_id_type=MESH,
     )
     couple_copy.start()
@@ -312,7 +326,7 @@
     for there, _, face in sides:
         @pl.when(jnp.logical_not(there))
         def _(face=face):
-            near_ref[face ^ 1] = jnp.zeros((2, 2 * K, M), F32)
+            near_ref[face ^ 1] = jnp.zeros((4, K, M), F32)
 
     load_face.wait()
 
@@ -347,14 +361,14 @@
         if f == 2:
             mix_couples()
         there = sides[f][0]
-        for part in range(2):
+        for part in range(4):
             @pl.when(there)
             def _(f=f, part=part):
                 pltpu.make_async_remote_copy(
                     src_ref=own_ref.at[part],
                     dst_ref=near_ref.at[f, part],
-                    send_sem=send_sems.at[2 * f + part],
-                    recv_sem=recv_sems.at[2 * f + part],
+                    send_sem=send_sems.at[4 * f + part],
+                    recv_sem=recv_sems.at[4 * f + part],
                     device_id=sides[f][1],
                     device_id_type=MESH,
                 ).wait_recv()
@@ -369,8 +383,8 @@
 
     def child_copy(i, source, target):
         return pltpu.make_async_remote_copy(
-            src_ref=source, dst_ref=target.at[odd], send_sem=send_sems.at[9 + i],
-            recv_sem=recv_sems.at[9 + i], device_id=partner, device_id_type=MESH,
+            src_ref=source, dst_ref=target.at[odd], send_sem=send_sems.at[17 + i],
+            recv_sem=recv_sems.at[17 + i], device_id=partner, device_id_type=MESH,
         )
 
     w_copy = child_copy(0, send_w, child_w)
@@ -420,7 +434,7 @@
         [count_two[0, 0, k] for k in range(parents)], write_two,
     )
 
-    for part in range(2):
+    for part in range(4):
         for there, copy in copies(part):
             @pl.when(there)
             def _(copy=copy):
@@ -433,7 +447,7 @@
 def shards(sizes, blocks, face_maps, *others):
     vmem = pl.BlockSpec(memory_space=pltpu.VMEM)
     hbm = pl.BlockSpec(memory_space=pltpu.HBM)
-    return pl.pallas_call(
+    results = pl.pallas_call(
         functools.partial(kernel, sizes),
         out_shape=(
             jax.ShapeDtypeStruct((1, 1, 8, K, K), F32),
@@ -446,8 +460,8 @@
             pltpu.VMEM((6, K, M), F32),
             pltpu.VMEM((8, M, M), F32),
             pltpu.VMEM((12, M, M), BF),
-            pltpu.VMEM((2, 2 * K, M), F32),
-            pltpu.VMEM((4, 2, 2 * K, M), F32),
+            pltpu.VMEM((4, K, M), F32),
+            pltpu.VMEM((4, 4, K, M), F32),
             pltpu.VMEM((4, M, M), F32),
             pltpu.VMEM((4, M, M), F32),
             pltpu.VMEM((4, M, M), F32),
@@ -466,14 +480,37 @@
             pltpu.SMEM((1, 1, 4), jnp.int32),
             pltpu.SMEM((1, 1, 8), jnp.int32),
             pltpu.SemaphoreType.DMA((15,)),
-            pltpu.SemaphoreType.DMA((11,)),
-            pltpu.SemaphoreType.DMA((11,)),
+            pltpu.SemaphoreType.DMA((19,)),
+            pltpu.SemaphoreType.DMA((19,)),
         ],
         compiler_params=pltpu.CompilerParams(
             collective_id=0, has_side_effects=True, vmem_limit_bytes=56 << 20
         ),
         name="factor",
     )(blocks, jnp.swapaxes(face_maps, 1, 2), *others)
+    return pl.pallas_call(
+        forward,
+        out_shape=tuple(jax.ShapeDtypeStruct(x.shape, F32) for x in results),
+        in_specs=[hbm] * 2,
+        out_specs=(hbm, hbm),
+        scratch_shapes=[pltpu.VMEM(x.shape, F32) for x in results]
+        + [pltpu.SemaphoreType.DMA((4,))],
+        compiler_params=pltpu.CompilerParams(vmem_limit_bytes=56 << 20),
+        name="forward",
+    )(*results)
+
+
+def forward(one, two, out_one, out_two, held_one, held_two, sems):
+    steps = ((one, held_one, out_one), (two, held_two, out_two))
+    reads = [pltpu.make_async_copy(a, b, sems.at[i]) for i, (a, b, _) in enumerate(steps)]
+    writes = [pltpu.make_async_copy(b, c, sems.at[2 + i]) for i, (_, b, c) in enumerate(steps)]
+    for read in reads:
+        read.start()
+    for read, write in zip(reads, writes):
+        read.wait()
+        write.start()
+    for write in writes:
+        write.wait()
 
 
 def solution(mesh):

time: 25.8 us -> 24.9 us (0.965)
  local copies, waits for them, and re-layouts: 2.37 us -> 0 us
  Pallas kernels: 22.7 us -> 24.2 us
    unnamed x4 -> x0, local copies, waits for them, and re-layouts: 2.37 us -> none
    pallas_call x0 -> x1, Pallas kernels: none -> 1.73 us  [shards(): pl.pallas_call(forward, out_shape=tuple((jax.ShapeDtypeStruct(x.shape, F3...]
    pallas_call x1, Pallas kernels: 22.7 us -> 22.4 us  [shards(): pl.pallas_call(functools.partial(kernel, sizes), out_shape=(jax.ShapeDtyp...]
where the time goes in v3:
time: 24.9 us; the launch traced here: 24.8 us
  Pallas kernels  24.2 us (97%)
  between operations  0.64 us (3%)
    pallas_call x1, Pallas kernels, shards(): pl.pallas_call(functools.partial(kernel, sizes), out_shape=(jax.ShapeDtyp...  22.4 us
    pallas_call x1, Pallas kernels, shards(): pl.pallas_call(forward, out_shape=tuple((jax.ShapeDtypeStruct(x.shape, F3...  1.73 us

profile of v3, /device:TPU:121, one launch (start us, length us, event | category | flops | bytes accessed | tf_op | source)
XLA Modules:
  0.0 24.8 jit_solution(16832489801827881381)
XLA Ops:
  0.6 22.4 %factor.1 = (f32[1,1,8,64,64]{4,3,2,1,0:T(8,128)}, f32[1,1,4,64,64]{4,3,2,1,0:T(8,128)}) custom-call(f32[1,1,8,128,128]{4,3,2,1,0:T(8,128)} %blocks_hbm.1, f32[6,64,128]{2,1,0:T(8,128)} %bitcast.1, f32[1,1,8,128,128]{4,3,2,1,0:T(8,128)} %couple_hbm.1, s32[1,1,8,128]{3,2,1,0:T(8,128)} %small_a.1, s32[1,1,8]{2,1,0:T(1,128)} %small_b.1, s32[1,1,8]{2,1,0:T(1,128)} %small_c.1, ...), custom_call_target="tpu_custom_call" | custom-call | tf_op jit(solution)/shard_map/factor/pallas_call | solution.py:450
  23.1 1.7 %forward.1 = (f32[1,1,8,64,64]{4,3,2,1,0:T(8,128)}, f32[1,1,4,64,64]{4,3,2,1,0:T(8,128)}) custom-call(f32[1,1,8,64,64]{4,3,2,1,0:T(8,128)} %get-tuple-element.4.one, f32[1,1,4,64,64]{4,3,2,1,0:T(8,128)} %get-tuple-element.5.two), custom_call_target="tpu_custom_call" | custom-call | tf_op jit(solution)/shard_map/forward/pallas_call | solution.py:491

commit v4 on v3

--- a/solution.py
+++ b/solution.py
@@ -91,15 +91,20 @@
             terms = [one + two for one, two in zip(terms[::2], terms[1::2])]
         return value - terms[0]
 
-    c = [spread([tiles[0][0], tiles[1][0]], q)[0] for q in range(8)]
+    c = [spread([tiles[0][0], tiles[1][0]], q)[0] for q in range(8)] if n == 1 else []
     for t in range(8):
         here, first = divmod(8 * t, W)
         after, start = divmod(8 * t + 8, W)
         ahead = [
             spread([tiles[t][after], tiles[t + 1][after]], start + q) for q in range(8)
-        ] if t < 7 else []
+        ] if t < 7 and n == 1 else []
         others = [(t + 1 + step) % 8 for step in range(7)]
-        cols = [spread([tiles[i][here] for i in others], first + q) for q in range(8)]
+        if n == 1:
+            cols = [spread([tiles[i][here] for i in others], first + q) for q in range(8)]
+        else:
+            cols = [spread([tiles[t][here]] + [tiles[i][here] for i in others], first + q) for q in range(8)]
+            c = [got[0] for got in cols]
+            cols = [got[1:] for got in cols]
         unit = within == sub + first
         x = list(tiles[t])
         x[here] = jnp.where(
@@ -127,7 +132,7 @@
     ]
 
 
-def skeletonize(read_block, turn_of, counts, write, weigh=None, between=None):
+def skeletonize(read_block, turn_of, counts, write, weigh=None, between=None, ready=None):
     boxes = len(counts)
     row_of = iota((K, M), 0)
     lane_of = iota((K, M), 1)
@@ -137,6 +142,8 @@
     groups, sides, centres = [], [], []
     for g in range(0, boxes, 4):
         grams = []
+        if ready is not None:
+            ready(g)
         for r in range(4):
             ah, al = split(read_block(g + r))
             turn = turn_of(g + r)
@@ -200,13 +207,23 @@
         write(b, nt3(applied, twice) + pad)
 
 
+def build_turns(order, turn_ref):
+    boxes = order.shape[0]
+    orders = rows(order.astype(F32), jnp.zeros((16 - boxes, M), F32)).T
+    lane = iota((M, M), 1).astype(F32)
+    for b in range(boxes):
+        turn_ref[b] = shifted(
+            jnp.where(orders[:, b : b + 1] == lane, 1.0, 0.0).astype(BF), W * (b % 4)
+        )
+
+
 def kernel(
     sizes,
-    blocks_hbm, faces_hbm, couple_hbm, small_a, small_b, small_c, small_d, small_e,
-    out_one, out_two,
+    blocks_hbm, faces_hbm, couple_hbm, small_a, small_b, small_c,
+    z_hbm, parents_hbm,
     a_ref, face_ref, c_ref, turn_ref, own_ref, near_ref, send_c, near_c, mixed_ref,
     q_ref, child_w, child_z, send_w, send_z, level_w, level_z, cross_ref, parent_ref,
-    order_one, order_two, count_one, count_two, merge_map,
+    order_one, count_one, merge_map,
     load_sems, send_sems, recv_sems,
 ):
     nx, ny = sizes
@@ -222,8 +239,7 @@
         pltpu.make_async_copy(source, target, load_sems.at[10 + i])
         for i, (source, target) in enumerate(
             zip(
-                (small_a, small_b, small_c, small_d, small_e),
-                (order_one, count_one, merge_map, order_two, count_two),
+                (small_a, small_b, small_c), (order_one, count_one, merge_map)
             )
         )
     ]
@@ -247,16 +263,7 @@
 
     for load in small_loads:
         load.wait()
-    orders = rows(
-        order_one[0, 0].astype(F32), order_two[0, 0].astype(F32), jnp.zeros((4, M), F32)
-    ).T
-    lane = iota((M, M), 1).astype(F32)
-
-    def build_turn(b):
-        turn_ref[b] = shifted(jnp.where(orders[:, b : b + 1] == lane, 1.0, 0.0).astype(BF), W * (b % 4))
-
-    for b in range(boxes):
-        build_turn(b)
+    build_turns(order_one[0, 0], turn_ref)
 
     row_of = iota((K, M), 0)
     lane_of = iota((K, M), 1)
@@ -320,9 +327,6 @@
     )
     couple_copy.start()
 
-    for k in range(parents):
-        build_turn(boxes + k)
-
     for there, _, face in sides:
         @pl.when(jnp.logical_not(there))
         def _(face=face):
@@ -357,13 +361,10 @@
         edge = 0 if f == 4 else boxes - 1
         q_ref[edge // 2, f * K : f * K + K, M * (edge % 2) : M * (edge % 2) + M] = jnp.zeros((K, M), F32)
 
-    for f in range(4):
-        if f == 2:
-            mix_couples()
-        there = sides[f][0]
-        for part in range(4):
-            @pl.when(there)
-            def _(f=f, part=part):
+    def receive(f, first, last):
+        for part in range(first, last):
+            @pl.when(sides[f][0])
+            def _(part=part):
                 pltpu.make_async_remote_copy(
                     src_ref=own_ref.at[part],
                     dst_ref=near_ref.at[f, part],
@@ -372,14 +373,22 @@
                     device_id=sides[f][1],
                     device_id_type=MESH,
                 ).wait_recv()
-        q = project(f, near_ref[f].reshape(4 * K, M))
-        for p in range(4):
-            q_ref[p, f * K : f * K + K, :] = q[p * K : p * K + K]
-
-    for p in range(4):
-        d = nn3(all_faces, split(q_ref[p]))
-        for i in (0, 1):
-            a_ref[2 * p + i] = a_ref[2 * p + i] - d[:, M * i : M * i + M]
+        q = project(f, near_ref[f, first:last].reshape((last - first) * K, M))
+        for p in range(first, last):
+            q_ref[p, f * K : f * K + K, :] = q[(p - first) * K : (p - first) * K + K]
+
+    receive(0, 0, 4)
+    receive(1, 0, 4)
+    mix_couples()
+
+    def ready(g):
+        first = g // 2
+        receive(2, first, first + 2)
+        receive(3, first, first + 2)
+        for p in range(first, first + 2):
+            d = nn3(all_faces, split(q_ref[p]))
+            for i in (0, 1):
+                a_ref[2 * p + i] = a_ref[2 * p + i] - d[:, M * i : M * i + M]
 
     def child_copy(i, source, target):
         return pltpu.make_async_remote_copy(
@@ -402,15 +411,16 @@
 
     def write_one(b, z):
         level_z[b] = z
-        out_one[0, 0, b] = z[:, :K]
 
     skeletonize(
-        lambda b: a_ref[b], lambda b: turn_ref[b], counts, write_one, weigh, send_weights
+        lambda b: a_ref[b], lambda b: turn_ref[b], counts, write_one, weigh, send_weights, ready
     )
 
     for k in range(parents):
         send_z[k] = level_z[send_box[k]]
     z_copy.start()
+    stores = [pltpu.make_async_copy(level_z, z_hbm, load_sems.at[13])]
+    stores[0].start()
     for k in range(parents):
         child_z[odd, k] = level_z[keep_box[k]]
 
@@ -425,41 +435,71 @@
     for k in range(parents):
         parent_ref[k, :K] = jnp.where(left, child_z[0, k], cross_ref[0, k])
         parent_ref[k, K:] = jnp.where(left, cross_ref[1, k], child_z[1, k])
-
-    def write_two(k, z):
-        out_two[0, 0, k] = z[:, :K]
-
-    skeletonize(
-        lambda k: parent_ref[k], lambda k: turn_ref[boxes + k],
-        [count_two[0, 0, k] for k in range(parents)], write_two,
-    )
+        stores.append(
+            pltpu.make_async_copy(parent_ref.at[k], parents_hbm.at[k], load_sems.at[14 + k])
+        )
+        stores[-1].start()
 
     for part in range(4):
         for there, copy in copies(part):
             @pl.when(there)
             def _(copy=copy):
                 copy.wait_send()
+    for store in stores:
+        store.wait()
     couple_copy.wait_send()
     w_copy.wait_send()
     z_copy.wait_send()
 
 
-def shards(sizes, blocks, face_maps, *others):
+def second_level(
+    z_hbm, parents_hbm, order_hbm, count_hbm, one_hbm, out_two,
+    z_ref, parent_ref, order, count, turn_ref, one_ref, sems,
+):
+    loads = [
+        pltpu.make_async_copy(source, target, sems.at[i])
+        for i, (source, target) in enumerate((
+            (order_hbm, order), (count_hbm, count), (parents_hbm, parent_ref), (z_hbm, z_ref)
+        ))
+    ]
+    for load in loads:
+        load.start()
+    loads[0].wait()
+    loads[1].wait()
+    build_turns(order[0, 0], turn_ref)
+    loads[3].wait()
+    for b in range(8):
+        one_ref[0, 0, b] = z_ref[b][:, :K]
+    store = pltpu.make_async_copy(one_ref, one_hbm, sems.at[4])
+    store.start()
+    loads[2].wait()
+
+    def write(k, z):
+        out_two[0, 0, k] = z[:, :K]
+
+    skeletonize(
+        lambda k: parent_ref[k], lambda k: turn_ref[k],
+        [count[0, 0, k] for k in range(4)], write,
+    )
+    store.wait()
+
+
+def shards(sizes, blocks, face_maps, couple, order_one, count_one, merge_map, order_two, count_two):
     vmem = pl.BlockSpec(memory_space=pltpu.VMEM)
     hbm = pl.BlockSpec(memory_space=pltpu.HBM)
     results = pl.pallas_call(
         functools.partial(kernel, sizes),
         out_shape=(
-            jax.ShapeDtypeStruct((1, 1, 8, K, K), F32),
-            jax.ShapeDtypeStruct((1, 1, 4, K, K), F32),
+            jax.ShapeDtypeStruct((8, K, M), F32),
+            jax.ShapeDtypeStruct((4, M, M), F32),
         ),
-        in_specs=[hbm] * 8,
-        out_specs=(vmem, vmem),
+        in_specs=[hbm] * 6,
+        out_specs=(hbm, hbm),
         scratch_shapes=[
             pltpu.VMEM((8, M, M), F32),
             pltpu.VMEM((6, K, M), F32),
             pltpu.VMEM((8, M, M), F32),
-            pltpu.VMEM((12, M, M), BF),
+            pltpu.VMEM((8, M, M), BF),
             pltpu.VMEM((4, K, M), F32),
             pltpu.VMEM((4, 4, K, M), F32),
             pltpu.VMEM((4, M, M), F32),
@@ -475,11 +515,9 @@
             pltpu.VMEM((2, 4, K, M), F32),
             pltpu.VMEM((4, M, M), F32),
             pltpu.VMEM((1, 1, 8, M), jnp.int32),
-            pltpu.VMEM((1, 1, 4, M), jnp.int32),
             pltpu.SMEM((1, 1, 8), jnp.int32),
-            pltpu.SMEM((1, 1, 4), jnp.int32),
             pltpu.SMEM((1, 1, 8), jnp.int32),
-            pltpu.SemaphoreType.DMA((15,)),
+            pltpu.SemaphoreType.DMA((18,)),
             pltpu.SemaphoreType.DMA((19,)),
             pltpu.SemaphoreType.DMA((19,)),
         ],
@@ -487,30 +525,27 @@
             collective_id=0, has_side_effects=True, vmem_limit_bytes=56 << 20
         ),
         name="factor",
-    )(blocks, jnp.swapaxes(face_maps, 1, 2), *others)
+    )(blocks, jnp.swapaxes(face_maps, 1, 2), couple, order_one, count_one, merge_map)
     return pl.pallas_call(
-        forward,
-        out_shape=tuple(jax.ShapeDtypeStruct(x.shape, F32) for x in results),
-        in_specs=[hbm] * 2,
-        out_specs=(hbm, hbm),
-        scratch_shapes=[pltpu.VMEM(x.shape, F32) for x in results]
-        + [pltpu.SemaphoreType.DMA((4,))],
+        second_level,
+        out_shape=(
+            jax.ShapeDtypeStruct((1, 1, 8, K, K), F32),
+            jax.ShapeDtypeStruct((1, 1, 4, K, K), F32),
+        ),
+        in_specs=[hbm] * 4,
+        out_specs=(hbm, vmem),
+        scratch_shapes=[
+            pltpu.VMEM((8, K, M), F32),
+            pltpu.VMEM((4, M, M), F32),
+            pltpu.VMEM((1, 1, 4, M), jnp.int32),
+            pltpu.SMEM((1, 1, 4), jnp.int32),
+            pltpu.VMEM((4, M, M), BF),
+            pltpu.VMEM((1, 1, 8, K, K), F32),
+            pltpu.SemaphoreType.DMA((5,)),
+        ],
         compiler_params=pltpu.CompilerParams(vmem_limit_bytes=56 << 20),
-        name="forward",
-    )(*results)
-
-
-def forward(one, two, out_one, out_two, held_one, held_two, sems):
-    steps = ((one, held_one, out_one), (two, held_two, out_two))
-    reads = [pltpu.make_async_copy(a, b, sems.at[i]) for i, (a, b, _) in enumerate(steps)]
-    writes = [pltpu.make_async_copy(b, c, sems.at[2 + i]) for i, (_, b, c) in enumerate(steps)]
-    for read in reads:
-        read.start()
-    for read, write in zip(reads, writes):
-        read.wait()
-        write.start()
-    for write in writes:
-        write.wait()
+        name="second_level",
+    )(*results, order_two, count_two)
 
 
 def solution(mesh):

time: 24.9 us -> 25.1 us (level)
    pallas_call x1, Pallas kernels: 1.73 us -> 5.39 us  [shards(): pl.pallas_call(second_level, out_shape=(jax.ShapeDtypeStruct((1, 1, 8, K,...]
    pallas_call x1, Pallas kernels: 22.4 us -> 18.9 us  [shards(): pl.pallas_call(functools.partial(kernel, sizes), out_shape=(jax.ShapeDtyp...]
where the time goes in v4:
time: 25.1 us; the launch traced here: 24.9 us
  Pallas kernels  24.3 us (97%)
  between operations  0.64 us (3%)
    pallas_call x1, Pallas kernels, shards(): pl.pallas_call(functools.partial(kernel, sizes), out_shape=(jax.ShapeDtyp...  18.9 us
    pallas_call x1, Pallas kernels, shards(): pl.pallas_call(second_level, out_shape=(jax.ShapeDtypeStruct((1, 1, 8, K,...  5.39 us

profile of v4, /device:TPU:121, one launch (start us, length us, event | category | flops | bytes accessed | tf_op | source)
XLA Modules:
  0.0 24.9 jit_solution(15233840970701829823)
XLA Ops:
  0.6 18.9 %factor.1 = (f32[8,64,128]{2,1,0:T(8,128)}, f32[4,128,128]{2,1,0:T(8,128)}) custom-call(f32[1,1,8,128,128]{4,3,2,1,0:T(8,128)} %blocks_hbm.1, f32[6,64,128]{2,1,0:T(8,128)} %bitcast.1, f32[1,1,8,128,128]{4,3,2,1,0:T(8,128)} %couple_hbm.1, s32[1,1,8,128]{3,2,1,0:T(8,128)} %small_a.1, s32[1,1,8]{2,1,0:T(1,128)} %small_b.1, s32[1,1,8]{2,1,0:T(1,128)} %small_c.1), custom_call_target="tpu_custom_call" | custom-call | tf_op jit(solution)/shard_map/factor/pallas_call | solution.py:490
  19.5 5.4 %second_level.1 = (f32[1,1,8,64,64]{4,3,2,1,0:T(8,128)}, f32[1,1,4,64,64]{4,3,2,1,0:T(8,128)}) custom-call(f32[8,64,128]{2,1,0:T(8,128)} %get-tuple-element.4.z_hbm, f32[4,128,128]{2,1,0:T(8,128)} %get-tuple-element.5.parents_hbm, s32[1,1,4,128]{3,2,1,0:T(4,128)} %order_hbm.1, s32[1,1,4]{2,1,0:T(1,128)} %count_hbm.1), custom_call_target="tpu_custom_call" | custom-call | tf_op jit(solution)/shard_map/second_level/pallas_call | solution.py:529

commit v5 on v3

--- a/solution.py
+++ b/solution.py
@@ -91,15 +91,20 @@
             terms = [one + two for one, two in zip(terms[::2], terms[1::2])]
         return value - terms[0]
 
-    c = [spread([tiles[0][0], tiles[1][0]], q)[0] for q in range(8)]
+    c = [spread([tiles[0][0], tiles[1][0]], q)[0] for q in range(8)] if n == 1 else []
     for t in range(8):
         here, first = divmod(8 * t, W)
         after, start = divmod(8 * t + 8, W)
         ahead = [
             spread([tiles[t][after], tiles[t + 1][after]], start + q) for q in range(8)
-        ] if t < 7 else []
+        ] if t < 7 and n == 1 else []
         others = [(t + 1 + step) % 8 for step in range(7)]
-        cols = [spread([tiles[i][here] for i in others], first + q) for q in range(8)]
+        if n == 1:
+            cols = [spread([tiles[i][here] for i in others], first + q) for q in range(8)]
+        else:
+            cols = [spread([tiles[t][here]] + [tiles[i][here] for i in others], first + q) for q in range(8)]
+            c = [got[0] for got in cols]
+            cols = [got[1:] for got in cols]
         unit = within == sub + first
         x = list(tiles[t])
         x[here] = jnp.where(

time: 24.9 us -> 24.6 us (0.988)
  Pallas kernels: 24.2 us -> 23.8 us
    pallas_call x1, Pallas kernels: 22.4 us -> 22.1 us  [shards(): pl.pallas_call(functools.partial(kernel, sizes), out_shape=(jax.ShapeDtyp...]
where the time goes in v5:
time: 24.6 us; the launch traced here: 24.4 us
  Pallas kernels  23.8 us (97%)
  between operations  0.64 us (3%)
    pallas_call x1, Pallas kernels, shards(): pl.pallas_call(functools.partial(kernel, sizes), out_shape=(jax.ShapeDtyp...  22.1 us
    pallas_call x1, Pallas kernels, shards(): pl.pallas_call(forward, out_shape=tuple((jax.ShapeDtypeStruct(x.shape, F3...  1.73 us

profile of v5, /device:TPU:121, one launch (start us, length us, event | category | flops | bytes accessed | tf_op | source)
XLA Modules:
  0.0 24.4 jit_solution(12105633589477472757)
XLA Ops:
  0.6 22.1 %factor.1 = (f32[1,1,8,64,64]{4,3,2,1,0:T(8,128)}, f32[1,1,4,64,64]{4,3,2,1,0:T(8,128)}) custom-call(f32[1,1,8,128,128]{4,3,2,1,0:T(8,128)} %blocks_hbm.1, f32[6,64,128]{2,1,0:T(8,128)} %bitcast.1, f32[1,1,8,128,128]{4,3,2,1,0:T(8,128)} %couple_hbm.1, s32[1,1,8,128]{3,2,1,0:T(8,128)} %small_a.1, s32[1,1,8]{2,1,0:T(1,128)} %small_b.1, s32[1,1,8]{2,1,0:T(1,128)} %small_c.1, ...), custom_call_target="tpu_custom_call" | custom-call | tf_op jit(solution)/shard_map/factor/pallas_call | solution.py:455
  22.7 1.7 %forward.1 = (f32[1,1,8,64,64]{4,3,2,1,0:T(8,128)}, f32[1,1,4,64,64]{4,3,2,1,0:T(8,128)}) custom-call(f32[1,1,8,64,64]{4,3,2,1,0:T(8,128)} %get-tuple-element.4.one, f32[1,1,4,64,64]{4,3,2,1,0:T(8,128)} %get-tuple-element.5.two), custom_call_target="tpu_custom_call" | custom-call | tf_op jit(solution)/shard_map/forward/pallas_call | solution.py:496
